TPU v7x, 128 devices: a whole 4x4x4 slice. The times are simulated.
128 devices in a mesh: dp: 16 (over z, x_hi, core), tensor: 8 (over y, x_lo).
Axes of the slice: x: 4 (x_hi: 2, x_lo: 2; x = x_hi * 2 + x_lo), y: 4, z: 4, core: 2. Of those that a mesh axis runs over, the one named last changes fastest.
Arguments:
- layer_input: bfloat16 [4096, 4096], P(('dp', 'tensor')), may hold values from -24 to 24
- output_grad: bfloat16 [4096, 4096], P(('dp', 'tensor')), may hold values from -24 to 24
- gate_weight: bfloat16 [4096, 7168], P(None, 'tensor'), may hold values from -0.09375 to 0.09375
- up_weight: bfloat16 [4096, 7168], P(None, 'tensor'), may hold values from -0.09375 to 0.09375
- down_weight: bfloat16 [7168, 4096], P('tensor'), may hold values from -0.0625 to 0.0625
Outputs:
- input_grad: bfloat16 [4096, 4096], P(('dp', 'tensor'))
- gate_grad: bfloat16 [4096, 7168], P('dp', 'tensor')
- up_grad: bfloat16 [4096, 7168], P('dp', 'tensor')
- down_grad: bfloat16 [7168, 4096], P('tensor', 'dp')
All inputs are finite; a program needn't handle non-finite values.
Results may differ from a plain program's by a relative error of at most 0.019.
Values may be sent and summed in bfloat16 or wider, within the bound.
A program may use at most 192 MiB of HBM per device.

v0:
```python
import jax
import jax.numpy as jnp
from jax import lax
from jax.sharding import PartitionSpec as P


def times_transposed(left, right):
    return lax.dot_general(
        left, right, (((1,), (1,)), ((), ())), preferred_element_type=jnp.float32
    )


def transposed_times(left, right):
    return lax.dot_general(
        left, right, (((0,), (0,)), ((), ())), preferred_element_type=jnp.float32
    )


def block_pass(input_rows, outgrad_rows, gate_weight, up_weight, down_weight):
    input_tok, outgrad_tok = (
        lax.all_gather(input_rows, "tensor", axis=0, tiled=True),
        lax.all_gather(outgrad_rows, "tensor", axis=0, tiled=True),
    )
    gate_pre = jnp.dot(input_tok, gate_weight, preferred_element_type=jnp.float32)
    up_pre = jnp.dot(input_tok, up_weight, preferred_element_type=jnp.float32)
    sigma = jax.nn.sigmoid(gate_pre)
    swish = gate_pre * sigma
    hidden = (swish * up_pre).astype(jnp.bfloat16)
    hidden_grad = times_transposed(outgrad_tok, down_weight)
    gate_delta = (hidden_grad * up_pre * sigma * (1.0 + gate_pre * (1.0 - sigma))).astype(
        jnp.bfloat16
    )
    up_delta = (hidden_grad * swish).astype(jnp.bfloat16)
    input_part = lax.psum_scatter(
        (times_transposed(gate_delta, gate_weight) + times_transposed(up_delta, up_weight)).astype(
            jnp.bfloat16
        ),
        "tensor",
        scatter_dimension=0,
        tiled=True,
    )
    return (input_tok, outgrad_tok, hidden, gate_delta, up_delta, input_part)


def per_device(layer_input, output_grad, gate_weight, up_weight, down_weight):
    results = block_pass(layer_input, output_grad, gate_weight, up_weight, down_weight)
    input_tok, outgrad_tok, hidden, gate_delta, up_delta, input_grad = results
    gate_local = transposed_times(input_tok, gate_delta)
    up_local = transposed_times(input_tok, up_delta)
    down_local = transposed_times(hidden, outgrad_tok)
    gate_sum, up_sum, down_sum = (
        lax.psum_scatter(
            gate_local.astype(jnp.bfloat16), "dp", scatter_dimension=0, tiled=True
        ).astype(jnp.float32),
        lax.psum_scatter(
            up_local.astype(jnp.bfloat16), "dp", scatter_dimension=0, tiled=True
        ).astype(jnp.float32),
        lax.psum_scatter(
            down_local.astype(jnp.bfloat16), "dp", scatter_dimension=1, tiled=True
        ).astype(jnp.float32),
    )
    return (
        input_grad,
        gate_sum.astype(jnp.bfloat16),
        up_sum.astype(jnp.bfloat16),
        down_sum.astype(jnp.bfloat16),
    )


def solution(mesh):
    placed = (
        P(("dp", "tensor"), None),
        P(("dp", "tensor"), None),
        P(None, "tensor"),
        P(None, "tensor"),
        P("tensor", None),
    )
    return jax.shard_map(
        per_device,
        mesh=mesh,
        in_specs=placed,
        out_specs=(
            P(("dp", "tensor"), None),
            P("dp", "tensor"),
            P("dp", "tensor"),
            P("tensor", "dp"),
        ),
        check_vma=False,
    )
```

profile of v0, /device:TPU:1, one launch (start us, length us, event | category | flops | bytes accessed | tf_op | source)
XLA Modules:
  0.0 479.4 jit_solution(7703473399234259673)
XLA Ops:
  7.2 0.7 all-gather.5.cloned.1.call-update
  7.9 0.0 all-gather.3.cloned.1.call-start
  7.9 0.7 all-gather.3.cloned.1.call-update
  8.6 0.0 reduce-scatter.9.cloned.1.call-start
  8.7 56.1 %all-gather.5.cloned.1.call-done = bf16[256,4096]{1,0:T(8,128)(2,1)} async-done(((bf16[32,4096]{1,0:T(8,128)(2,1)}), bf16[256,4096]{1,0:T(8,128)(2,1)}) %all-gather.5.cloned.1.call-update) | async-done | bytes 2097168 | tf_op jit(solution)/shard_map/all_gather | solution.py:21
  64.8 6.2 %fusion.5 = f32[256,896]{1,0:T(8,128)S(1)} fusion(bf16[256,4096]{1,0:T(8,128)(2,1)} %all-gather.5.cloned.1.call-done, bf16[4096,896]{1,0:T(8,128)(2,1)} %param.7), kind=kOutput, calls=%fused_computation.12 | convolution fusion | flops 1879048192 | bytes 10354688 | tf_op jit(solution)/shard_map/dot_general | solution.py:24
  71.0 6.4 %fusion.4 = f32[256,896]{1,0:T(8,128)} fusion(bf16[256,4096]{1,0:T(8,128)(2,1)S(1)} %copy-done, bf16[4096,896]{1,0:T(8,128)(2,1)} %param.8), kind=kOutput, calls=%fused_computation.11 | convolution fusion | flops 1879048192 | bytes 10354688 | tf_op jit(solution)/shard_map/dot_general | solution.py:25
  77.4 40.4 %all-gather.3.cloned.1.call-done = bf16[256,4096]{1,0:T(8,128)(2,1)} async-done(((bf16[32,4096]{1,0:T(8,128)(2,1)}), bf16[256,4096]{1,0:T(8,128)(2,1)}) %all-gather.3.cloned.1.call-update) | async-done | bytes 2097168 | tf_op jit(solution)/shard_map/all_gather | solution.py:22
  117.8 7.2 %multiply_convert_fusion.1 = (bf16[256,896]{1,0:T(8,128)(2,1)S(1)}, bf16[256,896]{1,0:T(8,128)(2,1)}) fusion(f32[256,896]{1,0:T(8,128)S(1)} %fusion.5, f32[256,896]{1,0:T(8,128)} %fusion.4, bf16[256,4096]{1,0:T(8,128)(2,1)} %all-gather.3.cloned.1.call-done, bf16[896,4096]{1,0:T(8,128)(2,1)} %param.9), kind=kOutput, calls=%fused_computation.6 | convolution fusion | flops 1882030080 | bytes 12189696 | tf_op jit(solution)/shard_map/dot_general | solution.py:8
  125.0 5.1 %convert_bitcast_fusion = bf16[4096,896]{0,1:T(8,128)(2,1)} fusion(bf16[256,896]{1,0:T(8,128)(2,1)S(1)} %get-tuple-element.8, bf16[256,4096]{1,0:T(8,128)(2,1)S(1)} %copy-done), kind=kOutput, calls=%fused_computation | convolution fusion | flops 1882718208 | bytes 9895936 | tf_op jit(solution)/shard_map/dot_general | solution.py:14
  130.1 0.0 reduce-scatter.7.cloned.1.call-start
  130.2 6.1 %convert_bitcast_fusion.1 = bf16[4096,896]{0,1:T(8,128)(2,1)} fusion(bf16[256,896]{1,0:T(8,128)(2,1)} %get-tuple-element.9, bf16[256,4096]{1,0:T(8,128)(2,1)S(1)} %copy-done), kind=kOutput, calls=%fused_computation.1 | convolution fusion | flops 1882718208 | bytes 9895936 | tf_op jit(solution)/shard_map/dot_general | solution.py:14
  136.3 0.2 reduce-scatter.5.cloned.1.call-start
  136.5 0.8 copy-done.2
  137.2 5.9 %fusion.6 = f32[256,4096]{1,0:T(8,128)S(1)} fusion(bf16[256,896]{1,0:T(8,128)(2,1)S(1)} %copy-done.2, bf16[4096,896]{1,0:T(8,128)(2,1)} %param.7), kind=kOutput, calls=%fused_computation.13 | convolution fusion | flops 1879048192 | bytes 11993088 | tf_op jit(solution)/shard_map/dot_general | solution.py:8
  143.1 7.7 %fusion = bf16[256,4096]{1,0:T(8,128)(2,1)} fusion(f32[256,4096]{1,0:T(8,128)S(1)} %fusion.6, bf16[256,896]{1,0:T(8,128)(2,1)S(1)} %get-tuple-element.8, bf16[4096,896]{1,0:T(8,128)(2,1)} %param.8), kind=kOutput, calls=%fused_computation.4 | convolution fusion | flops 1881145344 | bytes 14090240 | tf_op jit(solution)/shard_map/dot_general | solution.py:8
  150.8 0.0 reduce-scatter.11.cloned.1.call-start
  150.9 6.4 %convolution_convert_fusion = bf16[896,4096]{1,0:T(8,128)(2,1)} fusion(bf16[256,4096]{1,0:T(8,128)(2,1)S(1)} %copy-done.1, f32[256,896]{1,0:T(8,128)} %fusion.4, f32[256,896]{1,0:T(8,128)S(1)} %fusion.5), kind=kOutput, calls=%fused_computation.2 | convolution fusion | flops 1884094464 | bytes 11272192 | tf_op jit(solution)/shard_map/dot_general | solution.py:14
  157.3 65.5 %reduce-scatter.9.cloned.1.call-done = bf16[256,896]{0,1:T(8,128)(2,1)} async-done(((bf16[4096,896]{0,1:T(8,128)(2,1)}), bf16[256,896]{0,1:T(8,128)(2,1)}) %reduce-scatter.9.cloned.1.call-update) | async-done | bytes 458768 | tf_op jit(solution)/shard_map/reduce_scatter | solution.py:55
  222.8 2.0 copy.10
  224.8 95.4 %reduce-scatter.7.cloned.1.call-done = bf16[256,896]{0,1:T(8,128)(2,1)} async-done(((bf16[4096,896]{0,1:T(8,128)(2,1)}), bf16[256,896]{0,1:T(8,128)(2,1)}) %reduce-scatter.7.cloned.1.call-update) | async-done | bytes 458768 | tf_op jit(solution)/shard_map/reduce_scatter | solution.py:52
  320.1 2.0 copy.9
  322.1 53.3 %reduce-scatter.5.cloned.1.call-done = bf16[32,4096]{1,0:T(8,128)(2,1)} async-done(((bf16[256,4096]{1,0:T(8,128)(2,1)}), bf16[32,4096]{1,0:T(8,128)(2,1)}) %reduce-scatter.5.cloned.1.call-update) | async-done | bytes 262160 | tf_op jit(solution)/shard_map/reduce_scatter | solution.py:34
  375.4 97.2 %reduce-scatter.11.cloned.1.call-done = bf16[896,256]{1,0:T(8,128)(2,1)} async-done(((bf16[896,4096]{1,0:T(8,128)(2,1)}), bf16[896,256]{1,0:T(8,128)(2,1)}) %reduce-scatter.11.cloned.1.call-update) | async-done | bytes 458768 | tf_op jit(solution)/shard_map/reduce_scatter | solution.py:58
  (10 shorter events, 0.1 us)
Async XLA Ops:
  7.2 57.6 %all-gather.5.cloned.1.call-start = ((), (), s32[]{:S(2)}) async-start(), calls=%async_computation.5 | async-start | bytes 2359296 | tf_op jit(solution)/shard_map/all_gather | solution.py:21
  7.9 109.9 %all-gather.3.cloned.1.call-start = ((), (), s32[]{:S(2)}) async-start(), calls=%async_computation.4 | async-start | bytes 2359296 | tf_op jit(solution)/shard_map/all_gather | solution.py:22
  8.6 214.1 %reduce-scatter.9.cloned.1.call-start = ((), (), s32[]{:S(2)}) async-start(), calls=%async_computation.8 | async-start | bytes 7798784 | tf_op jit(solution)/shard_map/reduce_scatter | solution.py:55
  64.8 6.2 %copy-start = (bf16[256,4096]{1,0:T(8,128)(2,1)S(1)}, bf16[256,4096]{1,0:T(8,128)(2,1)}, u32[]{:S(2)}) copy-start(bf16[256,4096]{1,0:T(8,128)(2,1)} %all-gather.5.cloned.1.call-done) | copy-start | bytes 6291460
  130.1 190.0 %reduce-scatter.7.cloned.1.call-start = ((), (), s32[]{:S(2)}) async-start(), calls=%async_computation.7 | async-start | bytes 7798784 | tf_op jit(solution)/shard_map/reduce_scatter | solution.py:52
  136.2 1.0 copy-start.2
  136.3 239.2 %reduce-scatter.5.cloned.1.call-start = ((), (), s32[]{:S(2)}) async-start(), calls=%async_computation.6 | async-start | bytes 2359296 | tf_op jit(solution)/shard_map/reduce_scatter | solution.py:34
  143.1 7.8 %copy-start.1 = (bf16[256,4096]{1,0:T(8,128)(2,1)S(1)}, bf16[256,4096]{1,0:T(8,128)(2,1)}, u32[]{:S(2)}) copy-start(bf16[256,4096]{1,0:T(8,128)(2,1)} %all-gather.3.cloned.1.call-done) | copy-start | bytes 6291460
  150.8 321.7 %reduce-scatter.11.cloned.1.call-start = ((), (), s32[]{:S(2)}) async-start(), calls=%async_computation.9 | async-start | bytes 7798784 | tf_op jit(solution)/shard_map/reduce_scatter | solution.py:58
Sparse Core Ops, SparseCore 0:
  9.6 55.0 all-gather.4
  66.4 51.3 all-gather.2
  130.2 92.5 reduce-scatter.8
  226.9 93.2 reduce-scatter.6
  323.0 52.4 reduce-scatter.4
  380.1 92.4 reduce-scatter.10
where the time goes:
time: 480 us; the launch traced here: 479 us
  waiting for transfers between devices  409 us (85%)
  matrix products  50.8 us (11%)
  between operations  14.1 us (3%)
    reduce_scatter x1, waiting for transfers between devices, per_device(): lax.psum_scatter(down_local.astype(jnp.bfloat16), 'dp', scatter_dimension...  97.2 us
    reduce_scatter x1, waiting for transfers between devices, per_device(): lax.psum_scatter(gate_local.astype(jnp.bfloat16), 'dp', scatter_dimension...  95.4 us
    reduce_scatter x1, waiting for transfers between devices, per_device(): lax.psum_scatter(up_local.astype(jnp.bfloat16), 'dp', scatter_dimension=0...  65.5 us
    all_gather x1, waiting for transfers between devices, block_pass(): lax.all_gather(input_rows, 'tensor', axis=0, tiled=True)  56.1 us
    reduce_scatter x1, waiting for transfers between devices, block_pass(): lax.psum_scatter((times_transposed(gate_delta, gate_weight) + times_trans...  53.3 us
    all_gather x1, waiting for transfers between devices, block_pass(): lax.all_gather(outgrad_rows, 'tensor', axis=0, tiled=True)  40.4 us
    dot_general x3, matrix products, times_transposed(): lax.dot_general(left, right, (((1,), (1,)), ((), ())), preferred_element_...  20.7 us
    dot_general x3, matrix products, transposed_times(): lax.dot_general(left, right, (((0,), (0,)), ((), ())), preferred_element_...  17.5 us
  transfers between devices with their start and end apart: 6, of which 6 were waited for; matrix products, arithmetic and copies ran while one was open for 9% of the time, Pallas kernels for 0%

commit v1 on v0

v1 whole, which is shorter than its diff:
```python
import jax
import jax.numpy as jnp
from jax import lax
from jax.experimental import pallas as pl
from jax.experimental.pallas import tpu as pltpu
from jax.sharding import PartitionSpec as P

MESH = pl.DeviceIdType.MESH
BF16, F32 = jnp.bfloat16, jnp.float32

D = 4096
F = 896
ROWS = 32
TOK = 512
HALF = 16
BLK = 256
CH = 128
NCH = F // CH


def times_transposed(left, right):
    return lax.dot_general(left, right, (((1,), (1,)), ((), ())), preferred_element_type=F32)


def times(left, right):
    return jnp.dot(left, right, preferred_element_type=F32)


def kernel(
    x_hbm, dy_hbm, gw_hbm, uw_hbm, dw_hbm,
    dx_out, gg_out, ug_out, dg_out,
    buf, sib, wgu, wd, ab, gu, ht, xt, gpart, dpart, r1g, r1d, r2g, r2d, dxs, dxr, gfin, ufin, dfin, dxfin,
    ag_send, ag_recv, w_sem, own_sem, sib_send, sib_recv, ht_send, ht_recv, gu_send, gu_recv,
    s1_send, s1_recv, s2_send, s2_recv, dx_send, dx_recv, out_sem,
):
    dp, t = lax.axis_index("dp"), lax.axis_index("tensor")
    c, xh, z = lax.rem(dp, 2), lax.rem(dp // 2, 2), dp // 4
    y, xl = t // 2, lax.rem(t, 2)
    x = 2 * xh + xl

    def wrap(v):
        return lax.rem(v + 4, 4)

    def dev(pz, px, py, pc):
        return ((pz * 2 + px // 2) * 2 + pc, py * 2 + lax.rem(px, 2))

    sibling = dev(z, x, y, 1 - c)
    z_next, z_prev = dev(wrap(z + 1), x, y, c), dev(wrap(z - 1), x, y, c)

    barrier = pltpu.get_barrier_semaphore()
    greeted = [(dp, lax.rem(t + o, 8)) for o in range(1, 8)]
    greeted += [dev(z, wrap(x + 2 * xl - 1), y, c), z_next, z_prev, sibling]
    for other in greeted:
        pl.semaphore_signal(barrier, inc=1, device_id=other, device_id_type=MESH)

    def rows(px, py, h):
        slot = (px // 2) * 8 + py * 2 + lax.rem(px, 2)
        return pl.ds(pl.multiple_of(slot * ROWS + h * HALF, HALF), HALF)

    own = pl.ds(pl.multiple_of((xh * 8 + t) * ROWS, ROWS), ROWS)
    own_copies = [
        pltpu.make_async_copy(src, buf.at[a, own, :], own_sem.at[a]) for a, src in enumerate((x_hbm, dy_hbm))
    ]
    for copy in own_copies:
        copy.start()
    for j in range(NCH):
        part = pl.ds(j * CH, CH)
        pltpu.make_async_copy(gw_hbm.at[:, part], wgu.at[:, pl.ds(j * 2 * CH, CH)], w_sem.at[0]).start()
        pltpu.make_async_copy(uw_hbm.at[:, part], wgu.at[:, pl.ds(j * 2 * CH + CH, CH)], w_sem.at[0]).start()
    wd_copy = pltpu.make_async_copy(dw_hbm, wd, w_sem.at[1])
    wd_copy.start()
    for copy in own_copies:
        copy.wait()
    pl.semaphore_wait(barrier, len(greeted))

    lo, hi, full = pl.ds(0, D // 2), pl.ds(D // 2, D // 2), pl.ds(0, D)
    offsets = (0, 1, -1, 2)

    def xfer(a, h, idx, du, dv, cols, ring, way):
        u, v = (x, y) if h == 0 else (y, x)
        bu, bv = wrap(u + du), wrap(v + dv)
        tu, tv = (wrap(u + way), v) if ring == 0 else (u, wrap(v + way))
        (bx, by), (tx, ty) = ((bu, bv), (tu, tv)) if h == 0 else ((bv, bu), (tv, tu))
        block = buf.at[a, rows(bx, by, h), cols]
        return pltpu.make_async_remote_copy(
            src_ref=block,
            dst_ref=block,
            send_sem=ag_send.at[a * 2 + h, idx],
            recv_sem=ag_recv.at[a * 2 + h, idx],
            device_id=dev(z, tx, ty, c),
            device_id_type=MESH,
        )

    def first_full(a, h, way, sent):
        return xfer(a, h, 0 if way == 1 else 1, 0 if sent else -way, 0, full, 0, way)

    def first_relay(a, h, way, sent):
        idx, cols = (2, lo) if way == 1 else (3, hi)
        return xfer(a, h, idx, -way if sent else 2, 0, cols, 0, way)

    def second_full(a, h, q, way, sent):
        return xfer(a, h, 4 + 4 * q + (0 if way == 1 else 1), offsets[q], 0 if sent else -way, full, 1, way)

    def second_relay(a, h, q, way, sent):
        idx, cols = (4 + 4 * q + 2, lo) if way == 1 else (4 + 4 * q + 3, hi)
        return xfer(a, h, idx, offsets[q], -way if sent else 2, cols, 1, way)

    def gather_step(a, step):
        for h in range(2):
            if step == 0:
                for way in (1, -1):
                    first_full(a, h, way, True).start()
                for way in (1, -1):
                    second_full(a, h, 0, way, True).start()
            elif step == 1:
                for way, q in ((1, 2), (-1, 1)):
                    first_full(a, h, way, False).wait_recv()
                    first_relay(a, h, way, True).start()
                    for to in (1, -1):
                        second_full(a, h, q, to, True).start()
            elif step == 2:
                for way in (1, -1):
                    second_full(a, h, 0, way, False).wait_recv()
                    second_relay(a, h, 0, way, True).start()
                for way in (1, -1):
                    first_relay(a, h, way, False).wait_recv()
                for to in (1, -1):
                    second_full(a, h, 3, to, True).start()
            elif step == 3:
                for q in (2, 1):
                    for way in (1, -1):
                        second_full(a, h, q, way, False).wait_recv()
                        second_relay(a, h, q, way, True).start()
            elif step == 4:
                for way in (1, -1):
                    second_full(a, h, 3, way, False).wait_recv()
                    second_relay(a, h, 3, way, True).start()
            else:
                for q in range(4):
                    for way in (1, -1):
                        second_relay(a, h, q, way, False).wait_recv()

    def gather_sent(a):
        for h in range(2):
            for way in (1, -1):
                first_full(a, h, way, True).wait_send()
                first_relay(a, h, way, True).wait_send()
                for q in range(4):
                    second_full(a, h, q, way, True).wait_send()
                    second_relay(a, h, q, way, True).wait_send()

    def columns(zb, pc):
        return pl.ds(pl.multiple_of(zb * 1024 + xh * 512 + pc * BLK, BLK), BLK)

    def sibling_columns(a):
        for zb in range(4):
            pltpu.make_async_remote_copy(
                src_ref=buf.at[a, :, columns(zb, 1 - c)],
                dst_ref=sib.at[a, :, pl.ds(zb * BLK, BLK)],
                send_sem=sib_send.at[a],
                recv_sem=sib_recv.at[a],
                device_id=sibling,
                device_id_type=MESH,
            ).start()

    def pre_chunk(j):
        wide = pl.ds(pl.multiple_of(j * 2 * CH, 2 * CH), 2 * CH)
        pre = times(buf[0], wgu[:, wide])
        gate_pre, up_pre = pre[:, :CH], pre[:, CH:]
        sigma = jax.nn.sigmoid(gate_pre)
        swish = gate_pre * sigma
        hidden = swish * up_pre
        ab[:, wide] = jnp.concatenate([up_pre * sigma * (1.0 + gate_pre * (1.0 - sigma)), swish], axis=1)
        part = pl.ds(pl.multiple_of(j * CH, CH), CH)
        ht[part, pl.ds(0, TOK)] = hidden.T.astype(BF16)
        pltpu.make_async_remote_copy(
            src_ref=ht.at[part, pl.ds(0, TOK)],
            dst_ref=ht.at[part, pl.ds(TOK, TOK)],
            send_sem=ht_send.at[0],
            recv_sem=ht_recv.at[0],
            device_id=sibling,
            device_id_type=MESH,
        ).start()

    def delta_chunk(j, width):
        n = width * CH
        hg = times_transposed(buf[1], wd[pl.ds(pl.multiple_of(j * CH, CH), n), :])
        for w in range(width):
            wide = pl.ds(pl.multiple_of((j + w) * 2 * CH, 2 * CH), 2 * CH)
            part = hg[:, w * CH : (w + 1) * CH]
            gu[pl.ds(0, TOK), wide] = (jnp.concatenate([part, part], axis=1) * ab[:, wide]).astype(BF16)
        wide = pl.ds(pl.multiple_of(j * 2 * CH, 2 * CH), 2 * n)
        pltpu.make_async_remote_copy(
            src_ref=gu.at[pl.ds(0, TOK), wide],
            dst_ref=gu.at[pl.ds(TOK, TOK), wide],
            send_sem=gu_send.at[0],
            recv_sem=gu_recv.at[0],
            device_id=sibling,
            device_id_type=MESH,
        ).start()

    def whole(ref, sem):
        return pltpu.make_async_copy(ref, ref, sem)

    gather_step(0, 0)
    gather_step(0, 1)
    gather_step(0, 2)
    gather_step(1, 0)
    gather_step(0, 3)
    gather_step(1, 1)
    gather_step(0, 4)
    gather_step(1, 2)
    gather_step(0, 5)
    sibling_columns(0)
    whole(wgu, w_sem.at[0]).wait()

    @pl.loop(0, 3)
    def _(j):
        pre_chunk(j)

    gather_step(1, 3)

    @pl.loop(3, NCH)
    def _(j):
        pre_chunk(j)

    gather_step(1, 4)

    whole(sib.at[0], sib_recv.at[0]).wait()

    @pl.loop(0, 4)
    def _(k):
        zb = lax.rem(z + k, 4)
        xt[k, :, pl.ds(0, TOK)] = buf[0, :, columns(zb, c)].T
        xt[k, :, pl.ds(TOK, TOK)] = sib[0, :, pl.ds(pl.multiple_of(zb * BLK, BLK), BLK)].T

    gather_step(1, 5)
    sibling_columns(1)
    wd_copy.wait()

    @pl.loop(0, NCH // 2)
    def _(j):
        delta_chunk(2 * j, 2)

    delta_chunk(NCH - 1, 1)

    def down_part(k):
        zb = lax.rem(z + k, 4)
        total = times(ht[:, pl.ds(0, TOK)], buf[1, :, columns(zb, c)])
        total += times(ht[:, pl.ds(TOK, TOK)], sib[1, :, pl.ds(pl.multiple_of(zb * BLK, BLK), BLK)])
        dpart[k] = total.astype(BF16)

    def gu_part(k):
        @pl.loop(0, NCH)
        def _(j):
            wide = pl.ds(pl.multiple_of(j * 2 * CH, 2 * CH), 2 * CH)
            gpart[k, :, wide] = times(xt[k], gu[:, wide]).astype(BF16)

    def first(part, received, i, way):
        size = part.shape[1] // 2
        half = pl.ds(0 if way == 1 else size, size)
        side = 0 if way == 1 else 1
        return pltpu.make_async_remote_copy(
            src_ref=part.at[2, half, :],
            dst_ref=received.at[side],
            send_sem=s1_send.at[i, side],
            recv_sem=s1_recv.at[i, side],
            device_id=z_next if way == 1 else z_prev,
            device_id_type=MESH,
        )

    def second(part, received, i, way):
        side = 0 if way == 1 else 1
        return pltpu.make_async_remote_copy(
            src_ref=part.at[1 if way == 1 else 3],
            dst_ref=received.at[side],
            send_sem=s2_send.at[i, side],
            recv_sem=s2_recv.at[i, side],
            device_id=z_next if way == 1 else z_prev,
            device_id_type=MESH,
        )

    def add_first(part, received, i):
        size = part.shape[1] // 2
        for way in (1, -1):
            side, k = (0, 1) if way == 1 else (1, 3)
            first(part, received, i, way).wait_recv()
            half = pl.ds(side * size, size)
            part[k, half, :] = (part[k, half, :].astype(F32) + received[side].astype(F32)).astype(BF16)
            second(part, received_2[i], i, way).start()

    received_2 = (r2d, r2g)
    whole(sib.at[1], sib_recv.at[1]).wait()
    whole(ht.at[:, pl.ds(TOK, TOK)], ht_recv.at[0]).wait()
    down_part(2)
    for way in (1, -1):
        first(dpart, r1d, 0, way).start()
    whole(gu.at[pl.ds(TOK, TOK), :], gu_recv.at[0]).wait()
    gu_part(2)
    for way in (1, -1):
        first(gpart, r1g, 1, way).start()
    down_part(1)
    down_part(3)
    add_first(dpart, r1d, 0)

    @pl.loop(0, D // 256)
    def _(n):
        strip = pl.ds(pl.multiple_of(n * 256, 256), 256)
        mine = gu[pl.ds(pl.multiple_of(xh * 256, 256), 256), :]
        dxs[:, strip] = times_transposed(mine, wgu[strip, :]).astype(BF16)

    def dx_rows(s):
        return pl.ds(pl.multiple_of(s * ROWS, ROWS), ROWS)

    def dx_copy(o):
        to = lax.rem(t + o, 8)
        return pltpu.make_async_remote_copy(
            src_ref=dxs.at[dx_rows(to), :],
            dst_ref=dxr.at[dx_rows(t), :],
            send_sem=dx_send.at[o],
            recv_sem=dx_recv.at[o],
            device_id=(dp, to),
            device_id_type=MESH,
        )

    for o in range(1, 8):
        dx_copy(o).start()

    gu_part(1)
    gu_part(3)
    add_first(gpart, r1g, 1)
    down_part(0)
    gu_part(0)

    for way in (1, -1):
        second(dpart, r2d, 0, way).wait_recv()
    dfin[...] = (dpart[0].astype(F32) + r2d[0].astype(F32) + r2d[1].astype(F32)).astype(BF16)
    outs = [pltpu.make_async_copy(dfin, dg_out, out_sem.at[0])]
    outs[0].start()

    for o in range(1, 8):
        dx_copy(o).wait_recv()
    total = dxs[dx_rows(t), :].astype(F32)
    for o in range(1, 8):
        total += dxr[dx_rows(lax.rem(t + 8 - o, 8)), :].astype(F32)
    dxfin[...] = total.astype(BF16)
    outs.append(pltpu.make_async_copy(dxfin, dx_out, out_sem.at[1]))
    outs[1].start()

    for way in (1, -1):
        second(gpart, r2g, 1, way).wait_recv()

    @pl.loop(0, NCH)
    def _(j):
        wide = pl.ds(pl.multiple_of(j * 2 * CH, 2 * CH), 2 * CH)
        part = pl.ds(pl.multiple_of(j * CH, CH), CH)
        total = gpart[0, :, wide].astype(F32) + r2g[0, :, wide].astype(F32) + r2g[1, :, wide].astype(F32)
        gfin[:, part] = total[:, :CH].astype(BF16)
        ufin[:, part] = total[:, CH:].astype(BF16)

    outs.append(pltpu.make_async_copy(gfin, gg_out, out_sem.at[2]))
    outs.append(pltpu.make_async_copy(ufin, ug_out, out_sem.at[3]))
    outs[2].start()
    outs[3].start()

    for a in range(2):
        gather_sent(a)
        whole(sib.at[a], sib_send.at[a]).wait()
    whole(ht.at[:, pl.ds(0, TOK)], ht_send.at[0]).wait()
    whole(gu.at[pl.ds(0, TOK), :], gu_send.at[0]).wait()
    for way in (1, -1):
        for part, r1, r2, i in ((dpart, r1d, r2d, 0), (gpart, r1g, r2g, 1)):
            first(part, r1, i, way).wait_send()
            second(part, r2, i, way).wait_send()
    for o in range(1, 8):
        dx_copy(o).wait_send()
    for copy in outs:
        copy.wait()


def per_device(layer_input, output_grad, gate_weight, up_weight, down_weight):
    dma = pltpu.SemaphoreType.DMA
    vmem = pltpu.VMEM
    return pl.pallas_call(
        kernel,
        out_shape=(
            jax.ShapeDtypeStruct((ROWS, D), BF16),
            jax.ShapeDtypeStruct((BLK, F), BF16),
            jax.ShapeDtypeStruct((BLK, F), BF16),
            jax.ShapeDtypeStruct((F, BLK), BF16),
        ),
        in_specs=[pl.BlockSpec(memory_space=pl.ANY)] * 5,
        out_specs=[pl.BlockSpec(memory_space=pl.ANY)] * 4,
        scratch_shapes=[
            vmem((2, TOK, D), BF16),
            vmem((2, TOK, 4 * BLK), BF16),
            vmem((D, 2 * F), BF16),
            vmem((F, D), BF16),
            vmem((TOK, 2 * F), F32),
            vmem((2 * TOK, 2 * F), BF16),
            vmem((F, 2 * TOK), BF16),
            vmem((4, BLK, 2 * TOK), BF16),
            vmem((4, BLK, 2 * F), BF16),
            vmem((4, F, BLK), BF16),
            vmem((2, BLK // 2, 2 * F), BF16),
            vmem((2, F // 2, BLK), BF16),
            vmem((2, BLK, 2 * F), BF16),
            vmem((2, F, BLK), BF16),
            vmem((8 * ROWS, D), BF16),
            vmem((8 * ROWS, D), BF16),
            vmem((BLK, F), BF16),
            vmem((BLK, F), BF16),
            vmem((F, BLK), BF16),
            vmem((ROWS, D), BF16),
            dma((4, 20)),
            dma((4, 20)),
            dma((2,)),
            dma((2,)),
            dma((2,)),
            dma((2,)),
            dma((1,)),
            dma((1,)),
            dma((1,)),
            dma((1,)),
            dma((2, 2)),
            dma((2, 2)),
            dma((2, 2)),
            dma((2, 2)),
            dma((8,)),
            dma((8,)),
            dma((4,)),
        ],
        compiler_params=pltpu.CompilerParams(
            collective_id=0, has_side_effects=True, vmem_limit_bytes=63 * 1024 * 1024
        ),
        cost_estimate=pl.CostEstimate(flops=21 * 10**9, bytes_accessed=26 * 10**6, transcendentals=10**6),
    )(layer_input, output_grad, gate_weight, up_weight, down_weight)


def solution(mesh):
    placed = (
        P(("dp", "tensor"), None),
        P(("dp", "tensor"), None),
        P(None, "tensor"),
        P(None, "tensor"),
        P("tensor", None),
    )
    return jax.shard_map(
        per_device,
        mesh=mesh,
        in_specs=placed,
        out_specs=(
            P(("dp", "tensor"), None),
            P("dp", "tensor"),
            P("dp", "tensor"),
            P("tensor", "dp"),
        ),
        check_vma=False,
    )
```

time: 480 us -> 125 us (0.26)
  waiting for transfers between devices: 409 us -> 0 us
  Pallas kernels: 0 us -> 117 us
  matrix products: 50.8 us -> 0 us
  between operations: 14.1 us -> 0.64 us
    reduce_scatter x4 -> x0, waiting for transfers between devices: 311 us -> none  [the longest x1 97.2 us: per_device(): lax.psum_scatter(down_local.astype(jnp.bfloat16), 'dp', scatter_dimension...]
    pallas_call x0 -> x1, Pallas kernels: none -> 117 us  [per_device(): pl.pallas_call(kernel, out_shape=(jax.ShapeDtypeStruct((ROWS, D), BF16),...]
    all_gather x2 -> x0, waiting for transfers between devices: 96.5 us -> none  [the longest x1 56.1 us: block_pass(): lax.all_gather(input_rows, 'tensor', axis=0, tiled=True)]
    dot_general x8 -> x0, matrix products: 50.8 us -> none  [the longest x3 20.7 us: times_transposed(): lax.dot_general(left, right, (((1,), (1,)), ((), ())), preferred_element_...]
  transfers between devices with their start and end apart: 6 -> 0, of which waited for: 6 -> 0; matrix products, arithmetic and copies ran while one was open for 9% -> 0% of each run, Pallas kernels for 0% -> 0%
where the time goes in v1:
time: 125 us
  Pallas kernels  117 us (94%)
  local copies, waits for them, and re-layouts  7.13 us (6%)
    pallas_call x1, Pallas kernels, per_device(): pl.pallas_call(kernel, out_shape=(jax.ShapeDtypeStruct((ROWS, D), BF16),...  117 us
    unnamed x4, local copies, waits for them, and re-layouts  7.13 us

profile of v1, /device:TPU:1, one launch (start us, length us, event | category | flops | bytes accessed | tf_op | source)
XLA Modules:
  0.0 125.1 jit_solution(6455908958701070697)
XLA Ops:
  0.6 117.4 %shard_map.84 = (bf16[32,4096]{1,0:T(8,128)(2,1)}, bf16[256,896]{1,0:T(8,128)(2,1)}, bf16[256,896]{1,0:T(8,128)(2,1)}, bf16[896,256]{1,0:T(8,128)(2,1)}) custom-call(bf16[32,4096]{1,0:T(8,128)(2,1)} %x_hbm.1, bf16[32,4096]{1,0:T(8,128)(2,1)} %dy_hbm.1, bf16[4096,896]{1,0:T(8,128)(2,1)} %gw_hbm.1, bf16[4096,896]{1,0:T(8,128)(2,1)} %uw_hbm.1, ...), custom_call_target="tpu_custom_call" | custom-call | flops 20999999488 | bytes 26000000 | tf_op jit(solution)/shard_map/pallas_call | solution.py:384
  118.0 1.7 %copy.13 = bf16[32,4096]{1,0:T(8,128)(2,1)} copy(bf16[32,4096]{1,0:T(8,128)(2,1)} %get-tuple-element.8) | data formatting | bytes 524288
  119.7 1.8 %copy.14 = bf16[256,896]{1,0:T(8,128)(2,1)} copy(bf16[256,896]{1,0:T(8,128)(2,1)} %get-tuple-element.9) | data formatting | bytes 917504
  121.5 1.8 %copy.15 = bf16[256,896]{1,0:T(8,128)(2,1)} copy(bf16[256,896]{1,0:T(8,128)(2,1)} %get-tuple-element.10) | data formatting | bytes 917504
  123.3 1.8 %copy.16 = bf16[896,256]{1,0:T(8,128)(2,1)} copy(bf16[896,256]{1,0:T(8,128)(2,1)} %get-tuple-element.11) | data formatting | bytes 917504

commit v2 on v0

v2 whole, which is shorter than its diff:
```python
import jax
import jax.numpy as jnp
from jax import lax
from jax.experimental import pallas as pl
from jax.experimental.pallas import tpu as pltpu
from jax.sharding import PartitionSpec as P

MESH = pl.DeviceIdType.MESH
BF16, F32 = jnp.bfloat16, jnp.float32

D = 4096
F = 896
ROWS = 32
TOK = 512
HALF = 16
BLK = 256
CH = 128
NCH = F // CH
WIDE = D // 2


def times_transposed(left, right):
    return lax.dot_general(left, right, (((1,), (1,)), ((), ())), preferred_element_type=F32)


def times(left, right):
    return jnp.dot(left, right, preferred_element_type=F32)


def kernel(
    x_hbm, dy_hbm, gw_hbm, uw_hbm, dw_hbm,
    dx_out, gg_out, ug_out, dg_out,
    buf, sib, wgu, wd, ab, hga, gu, ht, xt, dpart, gpart, r1d, r1g, r2d, r2g, dxs, dxr, gfin, ufin,
    ag_send, ag_recv, w_sem, own_sem, sib_send, sib_recv, ht_send, ht_recv, gu_send, gu_recv,
    s1_send, s1_recv, s2_send, s2_recv, dx_send, dx_recv, out_sem,
):
    dp, t = lax.axis_index("dp"), lax.axis_index("tensor")
    c, xh, z = lax.rem(dp, 2), lax.rem(dp // 2, 2), dp // 4
    y, xl = t // 2, lax.rem(t, 2)
    x = 2 * xh + xl

    def wrap(v):
        return lax.rem(v + 4, 4)

    def dev(pz, px, py, pc):
        return ((pz * 2 + px // 2) * 2 + pc, py * 2 + lax.rem(px, 2))

    sibling = dev(z, x, y, 1 - c)
    z_next, z_prev = dev(wrap(z + 1), x, y, c), dev(wrap(z - 1), x, y, c)

    barrier = pltpu.get_barrier_semaphore()
    greeted = [(dp, lax.rem(t + o, 8)) for o in range(1, 8)]
    greeted += [dev(z, wrap(x + 2 * xl - 1), y, c), z_next, z_prev, sibling]
    for other in greeted:
        pl.semaphore_signal(barrier, inc=1, device_id=other, device_id_type=MESH)

    def rows(px, py, h):
        slot = (px // 2) * 8 + py * 2 + lax.rem(px, 2)
        return pl.ds(pl.multiple_of(slot * ROWS + h * HALF, HALF), HALF)

    own = pl.ds(pl.multiple_of((xh * 8 + t) * ROWS, ROWS), ROWS)
    own_copies = [
        pltpu.make_async_copy(src, buf.at[a, own, :], own_sem.at[a]) for a, src in enumerate((x_hbm, dy_hbm))
    ]
    for copy in own_copies:
        copy.start()
    for copy in own_copies:
        copy.wait()
    pl.semaphore_wait(barrier, len(greeted))

    wd_copy = pltpu.make_async_copy(dw_hbm, wd, w_sem.at[1])

    def load_weights():
        for j in range(NCH):
            part = pl.ds(j * CH, CH)
            pltpu.make_async_copy(gw_hbm.at[:, part], wgu.at[:, pl.ds(j * 2 * CH, CH)], w_sem.at[0]).start()
            pltpu.make_async_copy(uw_hbm.at[:, part], wgu.at[:, pl.ds(j * 2 * CH + CH, CH)], w_sem.at[0]).start()
        wd_copy.start()

    far = lax.rem(z + 2, 4)
    pair = far // 2
    units = ((0, 0, WIDE), (0, WIDE, WIDE), (1, far * 1024, 1024), (1, (4 * pair + 1 - far) * 1024, 1024), (1, (1 - pair) * WIDE, WIDE))
    offsets = (0, 1, -1, 2)

    def aligned(start, size):
        return pl.ds(start if isinstance(start, int) else pl.multiple_of(start, 256), size)

    def unit_columns(g, part):
        _, begin, size = units[g]
        return aligned(begin, size) if part is None else aligned(begin + part * (size // 2), size // 2)

    def xfer(g, h, idx, du, dv, part, ring, way):
        u, v = (x, y) if h == 0 else (y, x)
        bu, bv = wrap(u + du), wrap(v + dv)
        tu, tv = (wrap(u + way), v) if ring == 0 else (u, wrap(v + way))
        (bx, by), (tx, ty) = ((bu, bv), (tu, tv)) if h == 0 else ((bv, bu), (tv, tu))
        block = buf.at[units[g][0], rows(bx, by, h), unit_columns(g, part)]
        return pltpu.make_async_remote_copy(
            src_ref=block,
            dst_ref=block,
            send_sem=ag_send.at[g * 2 + h],
            recv_sem=ag_recv.at[g * 2 + h, idx],
            device_id=dev(z, tx, ty, c),
            device_id_type=MESH,
        )

    def first_full(g, h, way, sent):
        return xfer(g, h, 0 if way == 1 else 1, 0 if sent else -way, 0, None, 0, way)

    def first_relay(g, h, way, sent):
        idx, part = (2, 0) if way == 1 else (3, 1)
        return xfer(g, h, idx, -way if sent else 2, 0, part, 0, way)

    def second_full(g, h, q, way, sent):
        return xfer(g, h, 4 + 4 * q + (0 if way == 1 else 1), offsets[q], 0 if sent else -way, None, 1, way)

    def second_relay(g, h, q, way, sent):
        idx, part = (4 + 4 * q + 2, 0) if way == 1 else (4 + 4 * q + 3, 1)
        return xfer(g, h, idx, offsets[q], -way if sent else 2, part, 1, way)

    def gather(*acts):
        for g, h, what in acts:
            if what == 0:
                for way in (1, -1):
                    first_full(g, h, way, True).start()
                for way in (1, -1):
                    second_full(g, h, 0, way, True).start()
            elif what < 3:
                way, q = ((1, 2), (-1, 1))[what - 1]
                first_full(g, h, way, False).wait_recv()
                first_relay(g, h, way, True).start()
                for to in (1, -1):
                    second_full(g, h, q, to, True).start()
            elif what == 3:
                for way in (1, -1):
                    first_relay(g, h, way, False).wait_recv()
                for to in (1, -1):
                    second_full(g, h, 3, to, True).start()
            elif what < 12:
                q, way = (what - 4) // 2, 1 - 2 * (what % 2)
                second_full(g, h, q, way, False).wait_recv()
                second_relay(g, h, q, way, True).start()
            else:
                for q in range(4):
                    for way in (1, -1):
                        second_relay(g, h, q, way, False).wait_recv()

    def whole(ref, sem):
        return pltpu.make_async_copy(ref, ref, sem)

    def columns(zb, pc):
        return pl.ds(pl.multiple_of(zb * 1024 + xh * 512 + pc * BLK, BLK), BLK)

    def own_strip(zb):
        return pl.ds(pl.multiple_of(zb * BLK, BLK), BLK)

    def strips(g):
        a, begin, size = units[g]
        return [begin // 1024 + i for i in range(size // 1024)]

    def sibling_columns(g):
        for zb in strips(g):
            pltpu.make_async_remote_copy(
                src_ref=buf.at[units[g][0], :, columns(zb, 1 - c)],
                dst_ref=sib.at[units[g][0], :, own_strip(zb)],
                send_sem=sib_send.at[g],
                recv_sem=sib_recv.at[g],
                device_id=sibling,
                device_id_type=MESH,
            ).start()

    def sibling_wait(g, sem):
        a, begin, size = units[g]
        whole(sib.at[a, :, aligned(begin // 4, size // 4)], sem.at[g]).wait()

    def chunk(j):
        return pl.ds(pl.multiple_of(j * 2 * CH, 2 * CH), 2 * CH)

    pieces = ((0, 3), (3, 5), (5, 7))

    def pre_first(piece):
        j0, j1 = pieces[piece]
        if piece == 0:
            whole(wgu, w_sem.at[0]).wait()
        at = pl.ds(j0 * 2 * CH, (j1 - j0) * 2 * CH)
        ab[:, at] = times(buf[0, :, :WIDE], wgu[:WIDE, at])

    def pre_second(piece):
        j0, j1 = pieces[piece]
        at = pl.ds(j0 * 2 * CH, (j1 - j0) * 2 * CH)
        pre = ab[:, at] + times(buf[0, :, WIDE:], wgu[WIDE:, at])
        for j in range(j0, j1):
            begin = (j - j0) * 2 * CH
            gate_pre, up_pre = pre[:, begin : begin + CH], pre[:, begin + CH : begin + 2 * CH]
            sigma = jax.nn.sigmoid(gate_pre)
            swish = gate_pre * sigma
            hidden = swish * up_pre
            ab[:, chunk(j)] = jnp.concatenate([up_pre * sigma * (1.0 + gate_pre * (1.0 - sigma)), swish], axis=1)
            ht[pl.ds(j * CH, CH), pl.ds(0, TOK)] = hidden.T.astype(BF16)
        part = pl.ds(j0 * CH, (j1 - j0) * CH)
        pltpu.make_async_remote_copy(
            src_ref=ht.at[part, pl.ds(0, TOK)],
            dst_ref=ht.at[part, pl.ds(TOK, TOK)],
            send_sem=ht_send.at[0],
            recv_sem=ht_recv.at[0],
            device_id=sibling,
            device_id_type=MESH,
        ).start()

    def first_hidden_grad(piece):
        at, half = ((pl.ds(0, 512), pl.ds(512, 384))[piece], aligned(pair * WIDE, WIDE))
        if piece == 0:
            wd_copy.wait()
        hga[:, at] = times_transposed(buf[1, :, half], wd[at, half])

    def delta_size(i):
        return min(2, NCH - 2 * i) * CH

    def delta_chunk(i):
        at, half = pl.ds(i * 2 * CH, delta_size(i)), aligned((1 - pair) * WIDE, WIDE)
        hg = hga[:, at] + times_transposed(buf[1, :, half], wd[at, half])
        for w in range(delta_size(i) // CH):
            part = hg[:, w * CH : (w + 1) * CH]
            to = chunk(2 * i + w)
            gu[pl.ds(0, TOK), to] = (jnp.concatenate([part, part], axis=1) * ab[:, to]).astype(BF16)
        delta_copy(i).start()

    def delta_columns(i):
        return pl.ds(i * 4 * CH, 2 * delta_size(i))

    def delta_copy(i):
        return pltpu.make_async_remote_copy(
            src_ref=gu.at[pl.ds(0, TOK), delta_columns(i)],
            dst_ref=gu.at[pl.ds(TOK, TOK), delta_columns(i)],
            send_sem=gu_send.at[i],
            recv_sem=gu_recv.at[i],
            device_id=sibling,
            device_id_type=MESH,
        )

    def transposed_x():
        sibling_wait(0, sib_recv)
        sibling_wait(1, sib_recv)

        @pl.loop(0, 4)
        def _(k):
            zb = lax.rem(z + k, 4)
            xt[k, :, pl.ds(0, TOK)] = buf[0, :, columns(zb, c)].T
            xt[k, :, pl.ds(TOK, TOK)] = sib[0, :, own_strip(zb)].T

    def down_part(k):
        zb = lax.rem(z + k, 4)
        total = times(ht[:, pl.ds(0, TOK)], buf[1, :, columns(zb, c)])
        total += times(ht[:, pl.ds(TOK, TOK)], sib[1, :, own_strip(zb)])
        dpart[k] = total.astype(BF16)

    def gu_part(i, k):
        gpart[k, :, delta_columns(i)] = times(xt[k], gu[:, delta_columns(i)]).astype(BF16)

    sums = [(dpart, r1d, r2d, pl.ds(0, BLK))] + [(gpart, r1g, r2g, delta_columns(i)) for i in range(4)]

    def z_side(side):
        return dev(wrap(z + 1 - 2 * side), x, y, c)

    def half_of(i, side):
        size = sums[i][0].shape[1] // 2
        return pl.ds(side * size if isinstance(side, int) else pl.multiple_of(side * size, size), size)

    def first(i, side):
        part, received, _, cols = sums[i]
        return pltpu.make_async_remote_copy(
            src_ref=part.at[2, half_of(i, side), cols],
            dst_ref=received.at[side, :, cols],
            send_sem=s1_send.at[i, side],
            recv_sem=s1_recv.at[i, side],
            device_id=z_side(side),
            device_id_type=MESH,
        )

    def second(i, side):
        part, _, received, cols = sums[i]
        return pltpu.make_async_remote_copy(
            src_ref=part.at[1 + 2 * side, :, cols],
            dst_ref=received.at[side, :, cols],
            send_sem=s2_send.at[i, side],
            recv_sem=s2_recv.at[i, side],
            device_id=z_side(side),
            device_id_type=MESH,
        )

    def add_first(i, side):
        part, received, _, cols = sums[i]
        first(i, side).wait_recv()
        k, half = 1 + 2 * side, half_of(i, side)
        part[k, half, cols] = (part[k, half, cols].astype(F32) + received[side, :, cols].astype(F32)).astype(BF16)
        second(i, side).start()

    def add_second(i):
        part, _, received, cols = sums[i]
        for side in range(2):
            second(i, side).wait_recv()
        total = part[0, :, cols].astype(F32) + received[0, :, cols].astype(F32)
        return total + received[1, :, cols].astype(F32)

    side_a = 1 - lax.rem(z, 2)
    side_b = 1 - side_a

    def down_far():
        whole(ht.at[:, pl.ds(TOK, TOK)], ht_recv.at[0]).wait()
        sibling_wait(2, sib_recv)
        down_part(2)
        first(0, 0).start()
        first(0, 1).start()

    def down_near():
        sibling_wait(3, sib_recv)
        down_part(1 + 2 * side_a)

    def gu_far(i):
        delta_copy(i).wait_recv()
        gu_part(i, 2)
        first(1 + i, 0).start()
        first(1 + i, 1).start()

    def gu_near(i):
        for side in range(2):
            gu_part(i, 1 + 2 * side)
        for side in range(2):
            add_first(1 + i, side)

    def dx_rows(s):
        return pl.ds(pl.multiple_of(s * ROWS, ROWS), ROWS)

    def dx_copy(o, half):
        to = lax.rem(t + o, 8)
        at = pl.ds(half * WIDE, WIDE)
        return pltpu.make_async_remote_copy(
            src_ref=dxs.at[dx_rows(to), at],
            dst_ref=dxr.at[dx_rows(t), at],
            send_sem=dx_send.at[half, o],
            recv_sem=dx_recv.at[half, o],
            device_id=(dp, to),
            device_id_type=MESH,
        )

    def dx_part(half):
        mine = gu[pl.ds(pl.multiple_of(xh * 256, 256), 256), :]
        for n in range(2):
            strip = pl.ds(half * WIDE + n * 1024, 1024)
            dxs[:, strip] = times_transposed(mine, wgu[strip, :]).astype(BF16)

        for o in range(1, 8):
            dx_copy(o, half).start()

    gather((0, 0, 0), (0, 1, 0), (1, 1, 0), (1, 0, 0))
    load_weights()
    gather((0, 0, 1), (0, 0, 2), (0, 0, 4), (0, 0, 5), (0, 1, 4), (0, 1, 5), (0, 1, 1), (0, 1, 2), (1, 1, 4))
    gather((1, 1, 5), (1, 1, 1), (1, 1, 2), (1, 0, 1), (1, 0, 2), (1, 0, 4), (1, 0, 5), (0, 0, 3), (0, 0, 8))
    gather((0, 0, 9), (0, 1, 8), (0, 1, 9), (0, 0, 6), (0, 0, 7), (2, 0, 0), (0, 1, 6), (0, 1, 7), (0, 1, 3))
    gather((2, 1, 0), (1, 1, 3), (1, 1, 8), (1, 1, 9), (1, 0, 8), (1, 0, 9), (3, 1, 0), (1, 1, 6), (1, 1, 7))
    gather((1, 0, 6), (1, 0, 7), (1, 0, 3), (3, 0, 0), (4, 0, 0), (0, 0, 10), (0, 0, 11), (2, 0, 1), (0, 1, 10))
    gather((0, 1, 11), (2, 0, 4), (2, 0, 5), (2, 0, 2), (2, 1, 4), (2, 1, 5), (2, 1, 1), (2, 1, 2), (1, 1, 10))
    gather((1, 1, 11), (3, 1, 1), (3, 1, 2), (3, 1, 4), (3, 1, 5), (4, 1, 0), (1, 0, 10), (1, 0, 11), (3, 0, 4))
    gather((3, 0, 5), (3, 0, 1), (3, 0, 2), (4, 0, 1), (4, 0, 4), (0, 0, 12), (4, 0, 5), (0, 1, 12))
    sibling_columns(0)
    pre_first(0)
    gather((2, 0, 8), (2, 0, 9), (2, 0, 3), (2, 1, 8), (2, 1, 9), (2, 0, 6), (2, 0, 7), (2, 1, 6), (1, 1, 12))
    gather((2, 1, 7), (2, 1, 3), (3, 1, 3), (4, 0, 2))
    pre_first(1)
    gather((3, 1, 8), (1, 0, 12))
    sibling_columns(1)
    gather((3, 1, 9), (3, 1, 6), (3, 1, 7), (4, 1, 1), (4, 1, 2))
    pre_first(2)
    gather((3, 0, 8), (3, 0, 9), (3, 0, 3), (3, 0, 6), (3, 0, 7), (4, 1, 4), (4, 1, 5))
    pre_second(0)
    gather((2, 1, 11), (2, 1, 10), (2, 0, 10), (2, 0, 11), (3, 1, 11), (3, 1, 10), (4, 0, 8), (4, 0, 9), (4, 0, 3))
    pre_second(1)
    gather((4, 1, 8), (4, 1, 9), (4, 0, 6), (4, 0, 7))
    pre_second(2)
    gather((3, 0, 10), (3, 0, 11), (4, 1, 3), (2, 1, 12), (4, 1, 6), (2, 0, 12))
    sibling_columns(2)
    gather((4, 1, 7))
    transposed_x()
    gather((3, 1, 12))
    down_far()
    gather((4, 0, 10), (4, 0, 11), (3, 0, 12))
    sibling_columns(3)
    first_hidden_grad(0)
    gather((4, 1, 10), (4, 1, 11))
    first_hidden_grad(1)
    gather((4, 0, 12))
    down_near()
    gather((4, 1, 12))
    sibling_columns(4)
    delta_chunk(0)
    delta_chunk(1)
    add_first(0, side_a)
    gu_far(0)
    delta_chunk(2)
    gu_far(1)
    delta_chunk(3)
    sibling_wait(4, sib_recv)
    down_part(1 + 2 * side_b)
    add_first(0, side_b)
    gu_far(2)
    gu_far(3)
    dx_part(0)
    gu_near(0)
    dx_part(1)
    gu_near(1)
    gu_near(2)
    gu_near(3)
    down_part(0)
    for i in range(4):
        gu_part(i, 0)

    for i in range(5):
        for side in range(2):
            first(i, side).wait_send()
    outs = [
        pltpu.make_async_copy(dpart.at[2], dg_out, out_sem.at[0]),
        pltpu.make_async_copy(dxs.at[dx_rows(t), :], dx_out, out_sem.at[1]),
        pltpu.make_async_copy(gfin, gg_out, out_sem.at[2]),
        pltpu.make_async_copy(ufin, ug_out, out_sem.at[3]),
    ]
    dpart[2] = add_second(0).astype(BF16)
    outs[0].start()

    def grads(i):
        total = add_second(1 + i)
        for w in range(delta_size(i) // CH):
            at = pl.ds((2 * i + w) * CH, CH)
            gfin[:, at] = total[:, 2 * w * CH : (2 * w + 1) * CH].astype(BF16)
            ufin[:, at] = total[:, (2 * w + 1) * CH : (2 * w + 2) * CH].astype(BF16)

    grads(0)
    grads(1)
    for half in range(2):
        for o in range(1, 8):
            dx_copy(o, half).wait_recv()
    total = dxs[dx_rows(t), :].astype(F32)
    for o in range(1, 8):
        total += dxr[dx_rows(lax.rem(t + o, 8)), :].astype(F32)
    dxs[dx_rows(t), :] = total.astype(BF16)
    outs[1].start()
    grads(2)
    grads(3)
    outs[2].start()
    outs[3].start()

    for g, (_, _, size) in enumerate(units):
        for h in range(2):
            whole(buf.at[0, pl.ds(0, 15 * HALF), pl.ds(0, size)], ag_send.at[g * 2 + h]).wait()
        sibling_wait(g, sib_send)
    whole(ht.at[:, pl.ds(0, TOK)], ht_send.at[0]).wait()
    for i in range(4):
        delta_copy(i).wait_send()
    for i in range(5):
        for side in range(2):
            second(i, side).wait_send()
    for half in range(2):
        for o in range(1, 8):
            dx_copy(o, half).wait_send()
    for copy in outs:
        copy.wait()


def hand_on(*refs):
    for given, result in zip(refs[:4], refs[4:]):
        result[...] = given[...]


def per_device(layer_input, output_grad, gate_weight, up_weight, down_weight):
    dma = pltpu.SemaphoreType.DMA
    vmem = pltpu.VMEM
    results = (
        jax.ShapeDtypeStruct((ROWS, D), BF16),
        jax.ShapeDtypeStruct((BLK, F), BF16),
        jax.ShapeDtypeStruct((BLK, F), BF16),
        jax.ShapeDtypeStruct((F, BLK), BF16),
    )
    found = pl.pallas_call(
        kernel,
        out_shape=results,
        in_specs=[pl.BlockSpec(memory_space=pl.ANY)] * 5,
        out_specs=[pl.BlockSpec(memory_space=pl.ANY)] * 4,
        scratch_shapes=[
            vmem((2, TOK, D), BF16),
            vmem((2, TOK, 4 * BLK), BF16),
            vmem((D, 2 * F), BF16),
            vmem((F, D), BF16),
            vmem((TOK, 2 * F), F32),
            vmem((TOK, F), F32),
            vmem((2 * TOK, 2 * F), BF16),
            vmem((F, 2 * TOK), BF16),
            vmem((4, BLK, 2 * TOK), BF16),
            vmem((4, F, BLK), BF16),
            vmem((4, BLK, 2 * F), BF16),
            vmem((2, F // 2, BLK), BF16),
            vmem((2, BLK // 2, 2 * F), BF16),
            vmem((2, F, BLK), BF16),
            vmem((2, BLK, 2 * F), BF16),
            vmem((8 * ROWS, D), BF16),
            vmem((8 * ROWS, D), BF16),
            vmem((BLK, F), BF16),
            vmem((BLK, F), BF16),
            dma((10,)),
            dma((10, 20)),
            dma((2,)),
            dma((2,)),
            dma((5,)),
            dma((5,)),
            dma((1,)),
            dma((1,)),
            dma((4,)),
            dma((4,)),
            dma((5, 2)),
            dma((5, 2)),
            dma((5, 2)),
            dma((5, 2)),
            dma((2, 8)),
            dma((2, 8)),
            dma((4,)),
        ],
        compiler_params=pltpu.CompilerParams(
            collective_id=0, has_side_effects=True, vmem_limit_bytes=63 * 1024 * 1024
        ),
        cost_estimate=pl.CostEstimate(flops=21 * 10**9, bytes_accessed=26 * 10**6, transcendentals=10**6),
    )(layer_input, output_grad, gate_weight, up_weight, down_weight)
    return pl.pallas_call(
        hand_on,
        out_shape=results,
        in_specs=[pl.BlockSpec(memory_space=pltpu.VMEM)] * 4,
        out_specs=[pl.BlockSpec(memory_space=pltpu.VMEM)] * 4,
        cost_estimate=pl.CostEstimate(flops=0, bytes_accessed=4 * 10**6, transcendentals=0),
    )(*found)


def solution(mesh):
    placed = (
        P(("dp", "tensor"), None),
        P(("dp", "tensor"), None),
        P(None, "tensor"),
        P(None, "tensor"),
        P("tensor", None),
    )
    return jax.shard_map(
        per_device,
        mesh=mesh,
        in_specs=placed,
        out_specs=(
            P(("dp", "tensor"), None),
            P("dp", "tensor"),
            P("dp", "tensor"),
            P("tensor", "dp"),
        ),
        check_vma=False,
    )
```

time: 480 us -> 108 us (0.23)
  waiting for transfers between devices: 409 us -> 0 us
  Pallas kernels: 0 us -> 108 us
  matrix products: 50.8 us -> 0 us
  between operations: 14.1 us -> 0.64 us
    reduce_scatter x4 -> x0, waiting for transfers between devices: 311 us -> none  [the longest x1 97.2 us: per_device(): lax.psum_scatter(down_local.astype(jnp.bfloat16), 'dp', scatter_dimension...]
    pallas_call x0 -> x2, Pallas kernels: none -> 108 us  [the longest x1 105 us: per_device(): pl.pallas_call(kernel, out_shape=results, in_specs=[pl.BlockSpec(memory_s...]
    all_gather x2 -> x0, waiting for transfers between devices: 96.5 us -> none  [the longest x1 56.1 us: block_pass(): lax.all_gather(input_rows, 'tensor', axis=0, tiled=True)]
    dot_general x8 -> x0, matrix products: 50.8 us -> none  [the longest x3 20.7 us: times_transposed(): lax.dot_general(left, right, (((1,), (1,)), ((), ())), preferred_element_...]
  transfers between devices with their start and end apart: 6 -> 0, of which waited for: 6 -> 0; matrix products, arithmetic and copies ran while one was open for 9% -> 0% of each run, Pallas kernels for 0% -> 0%
where the time goes in v2:
time: 108 us
  Pallas kernels  108 us (100%)
    pallas_call x1, Pallas kernels, per_device(): pl.pallas_call(kernel, out_shape=results, in_specs=[pl.BlockSpec(memory_s...  105 us
    pallas_call x1, Pallas kernels, per_device(): pl.pallas_call(hand_on, out_shape=results, in_specs=[pl.BlockSpec(memory_...  2.57 us

profile of v2, /device:TPU:1, one launch (start us, length us, event | category | flops | bytes accessed | tf_op | source)
XLA Modules:
  0.0 108.2 jit_solution(13244467059538853341)
XLA Ops:
  0.6 105.0 %shard_map.84 = (bf16[32,4096]{1,0:T(8,128)(2,1)}, bf16[256,896]{1,0:T(8,128)(2,1)}, bf16[256,896]{1,0:T(8,128)(2,1)}, bf16[896,256]{1,0:T(8,128)(2,1)}) custom-call(bf16[32,4096]{1,0:T(8,128)(2,1)} %x_hbm.1, bf16[32,4096]{1,0:T(8,128)(2,1)} %dy_hbm.1, bf16[4096,896]{1,0:T(8,128)(2,1)} %gw_hbm.1, bf16[4096,896]{1,0:T(8,128)(2,1)} %uw_hbm.1, ...), custom_call_target="tpu_custom_call" | custom-call | flops 20999999488 | bytes 26000000 | tf_op jit(solution)/shard_map/pallas_call | solution.py:482
  105.7 2.6 %shard_map.85 = (bf16[32,4096]{1,0:T(8,128)(2,1)}, bf16[256,896]{1,0:T(8,128)(2,1)}, bf16[256,896]{1,0:T(8,128)(2,1)}, bf16[896,256]{1,0:T(8,128)(2,1)}) custom-call(bf16[32,4096]{1,0:T(8,128)(2,1)} %get-tuple-element.8.refs_0_, bf16[256,896]{1,0:T(8,128)(2,1)} %get-tuple-element.9.refs_1_, bf16[256,896]{1,0:T(8,128)(2,1)} %get-tuple-element.10.refs_2_, ...), custom_call_target="tpu_custom_call" | custom-call | bytes 4000000 | tf_op jit(solution)/shard_map/pallas_call | solution.py:530

commit v3 on v2

--- a/solution.py
+++ b/solution.py
@@ -352,45 +352,42 @@
         for o in range(1, 8):
             dx_copy(o, half).start()
 
-    gather((0, 0, 0), (0, 1, 0), (1, 1, 0), (1, 0, 0))
+    gather((0, 0, 0), (0, 1, 0), (1, 0, 0), (1, 1, 0))
     load_weights()
-    gather((0, 0, 1), (0, 0, 2), (0, 0, 4), (0, 0, 5), (0, 1, 4), (0, 1, 5), (0, 1, 1), (0, 1, 2), (1, 1, 4))
-    gather((1, 1, 5), (1, 1, 1), (1, 1, 2), (1, 0, 1), (1, 0, 2), (1, 0, 4), (1, 0, 5), (0, 0, 3), (0, 0, 8))
-    gather((0, 0, 9), (0, 1, 8), (0, 1, 9), (0, 0, 6), (0, 0, 7), (2, 0, 0), (0, 1, 6), (0, 1, 7), (0, 1, 3))
-    gather((2, 1, 0), (1, 1, 3), (1, 1, 8), (1, 1, 9), (1, 0, 8), (1, 0, 9), (3, 1, 0), (1, 1, 6), (1, 1, 7))
-    gather((1, 0, 6), (1, 0, 7), (1, 0, 3), (3, 0, 0), (4, 0, 0), (0, 0, 10), (0, 0, 11), (2, 0, 1), (0, 1, 10))
-    gather((0, 1, 11), (2, 0, 4), (2, 0, 5), (2, 0, 2), (2, 1, 4), (2, 1, 5), (2, 1, 1), (2, 1, 2), (1, 1, 10))
-    gather((1, 1, 11), (3, 1, 1), (3, 1, 2), (3, 1, 4), (3, 1, 5), (4, 1, 0), (1, 0, 10), (1, 0, 11), (3, 0, 4))
-    gather((3, 0, 5), (3, 0, 1), (3, 0, 2), (4, 0, 1), (4, 0, 4), (0, 0, 12), (4, 0, 5), (0, 1, 12))
+    gather((0, 0, 1), (0, 0, 2), (0, 0, 4), (0, 0, 5), (0, 1, 4), (0, 1, 5), (0, 1, 1), (0, 1, 2), (1, 0, 2))
+    gather((1, 0, 1), (1, 1, 5), (1, 1, 4), (1, 0, 5), (1, 0, 4), (1, 1, 2), (1, 1, 1), (0, 0, 3), (0, 1, 3))
+    gather((2, 1, 0), (1, 0, 3), (0, 1, 8), (0, 1, 6), (0, 1, 9), (0, 1, 7), (0, 0, 9), (0, 0, 8), (0, 0, 7))
+    gather((0, 0, 6), (1, 1, 3), (2, 1, 5), (2, 1, 4), (2, 0, 0), (1, 0, 6), (1, 0, 7), (2, 1, 1), (2, 1, 2))
+    gather((1, 0, 8), (1, 0, 9), (1, 1, 7), (1, 1, 9), (1, 1, 6), (1, 1, 8), (3, 0, 0), (0, 1, 11), (0, 1, 10))
+    gather((4, 0, 0), (0, 0, 11), (0, 0, 10), (3, 1, 0), (2, 1, 3), (1, 0, 11), (1, 0, 10), (2, 0, 1), (2, 0, 2))
+    gather((2, 0, 5), (2, 0, 4), (4, 1, 0), (3, 0, 4), (3, 0, 5), (2, 1, 8), (2, 1, 6), (2, 1, 9), (2, 1, 7))
+    gather((0, 0, 12), (3, 0, 1), (3, 0, 2), (0, 1, 12))
     sibling_columns(0)
     pre_first(0)
-    gather((2, 0, 8), (2, 0, 9), (2, 0, 3), (2, 1, 8), (2, 1, 9), (2, 0, 6), (2, 0, 7), (2, 1, 6), (1, 1, 12))
-    gather((2, 1, 7), (2, 1, 3), (3, 1, 3), (4, 0, 2))
+    gather((1, 1, 10), (1, 1, 11), (1, 0, 12), (2, 0, 3), (2, 1, 11), (2, 1, 10), (2, 0, 9), (2, 0, 8), (3, 1, 1))
+    gather((3, 1, 2), (2, 0, 7), (2, 0, 6), (3, 1, 5), (3, 1, 4))
     pre_first(1)
-    gather((3, 1, 8), (1, 0, 12))
+    gather((3, 0, 3), (4, 0, 4), (4, 0, 5), (4, 0, 1), (4, 0, 2), (4, 1, 4), (4, 1, 5))
+    pre_first(2)
+    gather((3, 0, 8), (3, 0, 9), (3, 0, 6), (3, 0, 7), (4, 1, 1), (4, 1, 2), (2, 1, 12), (3, 1, 3), (1, 1, 12))
     sibling_columns(1)
-    gather((3, 1, 9), (3, 1, 6), (3, 1, 7), (4, 1, 1), (4, 1, 2))
-    pre_first(2)
-    gather((3, 0, 8), (3, 0, 9), (3, 0, 3), (3, 0, 6), (3, 0, 7), (4, 1, 4), (4, 1, 5))
     pre_second(0)
-    gather((2, 1, 11), (2, 1, 10), (2, 0, 10), (2, 0, 11), (3, 1, 11), (3, 1, 10), (4, 0, 8), (4, 0, 9), (4, 0, 3))
+    gather((2, 0, 11), (2, 0, 10), (3, 1, 8), (3, 1, 9), (3, 1, 6), (3, 1, 7), (4, 0, 3))
     pre_second(1)
-    gather((4, 1, 8), (4, 1, 9), (4, 0, 6), (4, 0, 7))
+    gather((3, 0, 11), (3, 0, 10), (3, 1, 10), (3, 1, 11), (4, 1, 3))
     pre_second(2)
-    gather((3, 0, 10), (3, 0, 11), (4, 1, 3), (2, 1, 12), (4, 1, 6), (2, 0, 12))
+    gather((4, 0, 8), (2, 0, 12))
     sibling_columns(2)
-    gather((4, 1, 7))
+    gather((4, 0, 9), (4, 0, 6), (4, 0, 7), (4, 1, 8), (4, 1, 6), (4, 1, 9), (4, 1, 7))
     transposed_x()
-    gather((3, 1, 12))
-    down_far()
-    gather((4, 0, 10), (4, 0, 11), (3, 0, 12))
+    gather((3, 0, 12), (3, 1, 12))
     sibling_columns(3)
     first_hidden_grad(0)
-    gather((4, 1, 10), (4, 1, 11))
+    gather((4, 0, 10), (4, 0, 11), (4, 1, 11), (4, 1, 10))
+    down_far()
+    down_near()
     first_hidden_grad(1)
-    gather((4, 0, 12))
-    down_near()
-    gather((4, 1, 12))
+    gather((4, 0, 12), (4, 1, 12))
     sibling_columns(4)
     delta_chunk(0)
     delta_chunk(1)

time: 108 us -> 108 us (level); the launches traced: 108 us -> 107 us
    pallas_call x1, Pallas kernels: 105 us -> 104 us  [per_device(): pl.pallas_call(kernel, out_shape=results, in_specs=[pl.BlockSpec(memory_s...]
where the time goes in v3:
time: 108 us; the launch traced here: 107 us
  Pallas kernels  107 us (99%)
    pallas_call x1, Pallas kernels, per_device(): pl.pallas_call(kernel, out_shape=results, in_specs=[pl.BlockSpec(memory_s...  104 us
    pallas_call x1, Pallas kernels, per_device(): pl.pallas_call(hand_on, out_shape=results, in_specs=[pl.BlockSpec(memory_...  2.57 us

profile of v3, /device:TPU:1, one launch (start us, length us, event | category | flops | bytes accessed | tf_op | source)
XLA Modules:
  0.0 107.1 jit_solution(11297958017520536239)
XLA Ops:
  0.6 103.9 %shard_map.84 = (bf16[32,4096]{1,0:T(8,128)(2,1)}, bf16[256,896]{1,0:T(8,128)(2,1)}, bf16[256,896]{1,0:T(8,128)(2,1)}, bf16[896,256]{1,0:T(8,128)(2,1)}) custom-call(bf16[32,4096]{1,0:T(8,128)(2,1)} %x_hbm.1, bf16[32,4096]{1,0:T(8,128)(2,1)} %dy_hbm.1, bf16[4096,896]{1,0:T(8,128)(2,1)} %gw_hbm.1, bf16[4096,896]{1,0:T(8,128)(2,1)} %uw_hbm.1, ...), custom_call_target="tpu_custom_call" | custom-call | flops 20999999488 | bytes 26000000 | tf_op jit(solution)/shard_map/pallas_call | solution.py:479
  104.6 2.6 %shard_map.85 = (bf16[32,4096]{1,0:T(8,128)(2,1)}, bf16[256,896]{1,0:T(8,128)(2,1)}, bf16[256,896]{1,0:T(8,128)(2,1)}, bf16[896,256]{1,0:T(8,128)(2,1)}) custom-call(bf16[32,4096]{1,0:T(8,128)(2,1)} %get-tuple-element.8.refs_0_, bf16[256,896]{1,0:T(8,128)(2,1)} %get-tuple-element.9.refs_1_, bf16[256,896]{1,0:T(8,128)(2,1)} %get-tuple-element.10.refs_2_, ...), custom_call_target="tpu_custom_call" | custom-call | bytes 4000000 | tf_op jit(solution)/shard_map/pallas_call | solution.py:527

commit v4 on v3

--- a/solution.py
+++ b/solution.py
@@ -182,16 +182,14 @@
         j0, j1 = pieces[piece]
         if piece == 0:
             whole(wgu, w_sem.at[0]).wait()
-        at = pl.ds(j0 * 2 * CH, (j1 - j0) * 2 * CH)
-        ab[:, at] = times(buf[0, :, :WIDE], wgu[:WIDE, at])
+        for j in range(j0, j1):
+            ab[:, chunk(j)] = times(buf[0, :, :WIDE], wgu[:WIDE, chunk(j)])
 
     def pre_second(piece):
         j0, j1 = pieces[piece]
-        at = pl.ds(j0 * 2 * CH, (j1 - j0) * 2 * CH)
-        pre = ab[:, at] + times(buf[0, :, WIDE:], wgu[WIDE:, at])
         for j in range(j0, j1):
-            begin = (j - j0) * 2 * CH
-            gate_pre, up_pre = pre[:, begin : begin + CH], pre[:, begin + CH : begin + 2 * CH]
+            pre = ab[:, chunk(j)] + times(buf[0, :, WIDE:], wgu[WIDE:, chunk(j)])
+            gate_pre, up_pre = pre[:, :CH], pre[:, CH:]
             sigma = jax.nn.sigmoid(gate_pre)
             swish = gate_pre * sigma
             hidden = swish * up_pre

time: 108 us -> 108 us (level)
  no operation moved by 1% of the time
where the time goes in v4:
time: 108 us; the launch traced here: 107 us
  Pallas kernels  107 us (99%)
    pallas_call x1, Pallas kernels, per_device(): pl.pallas_call(kernel, out_shape=results, in_specs=[pl.BlockSpec(memory_s...  104 us
    pallas_call x1, Pallas kernels, per_device(): pl.pallas_call(hand_on, out_shape=results, in_specs=[pl.BlockSpec(memory_...  2.57 us

profile of v4, /device:TPU:1, one launch (start us, length us, event | category | flops | bytes accessed | tf_op | source)
XLA Modules:
  0.0 107.1 jit_solution(11485115966182237748)
XLA Ops:
  0.6 103.9 %shard_map.84 = (bf16[32,4096]{1,0:T(8,128)(2,1)}, bf16[256,896]{1,0:T(8,128)(2,1)}, bf16[256,896]{1,0:T(8,128)(2,1)}, bf16[896,256]{1,0:T(8,128)(2,1)}) custom-call(bf16[32,4096]{1,0:T(8,128)(2,1)} %x_hbm.1, bf16[32,4096]{1,0:T(8,128)(2,1)} %dy_hbm.1, bf16[4096,896]{1,0:T(8,128)(2,1)} %gw_hbm.1, bf16[4096,896]{1,0:T(8,128)(2,1)} %uw_hbm.1, ...), custom_call_target="tpu_custom_call" | custom-call | flops 20999999488 | bytes 26000000 | tf_op jit(solution)/shard_map/pallas_call | solution.py:477
  104.6 2.6 %shard_map.85 = (bf16[32,4096]{1,0:T(8,128)(2,1)}, bf16[256,896]{1,0:T(8,128)(2,1)}, bf16[256,896]{1,0:T(8,128)(2,1)}, bf16[896,256]{1,0:T(8,128)(2,1)}) custom-call(bf16[32,4096]{1,0:T(8,128)(2,1)} %get-tuple-element.8.refs_0_, bf16[256,896]{1,0:T(8,128)(2,1)} %get-tuple-element.9.refs_1_, bf16[256,896]{1,0:T(8,128)(2,1)} %get-tuple-element.10.refs_2_, ...), custom_call_target="tpu_custom_call" | custom-call | bytes 4000000 | tf_op jit(solution)/shard_map/pallas_call | solution.py:525
